TPU v7x, 256 devices: a whole 4x4x8 slice. The times are simulated.
256 devices in a mesh: space: 128 (over y, z_lo, x, core), phase: 2 (over z_hi).
Axes of the slice: x: 4, y: 4, z: 8 (z_hi: 2, z_lo: 4; z = z_hi * 4 + z_lo), core: 2. Of those that a mesh axis runs over, the one named last changes fastest.
Arguments:
- particle_cell: int32 [2, 8192, 128], P('phase', 'space'), may hold values from 0 to 63
- block_count: int32 [2, 8192], P('phase', 'space'), may hold values from 1 to 128, as said below
- particle_frac: float32 [2, 3, 8192, 128], P('phase', None, 'space'), may hold values from 0 to 1
- particle_vel: float32 [2, 3, 8192, 128], P('phase', None, 'space'), may hold values from -2.5 to 2.5
- particle_mass: float32 [2, 8192, 128], P('phase', 'space'), may hold values from 0.5 to 2
- particle_stress: float32 [2, 8192, 128], P('phase', 'space'), may hold values from -6 to 6
- drag_coef: float32 [512, 8, 128], P('space'), may hold values from 0.2 to 5
Outputs:
- frac_out: float32 [2, 3, 8192, 128], P('phase', None, 'space')
- vel_out: float32 [2, 3, 8192, 128], P('phase', None, 'space')
- stress_out: float32 [2, 8192, 128], P('phase', 'space')
Inputs may be any that keep to these rules, and one draw needn't show every extreme that they name: `particle_cell`: the cell of a slot within its block of 4 x 4 x 4 cells, numbered 16 a + 4 b + c for the offsets a, b, c along the first, second and third dimension. `block_count`: slots 0 to count - 1 of a block hold particles, the others are empty; among the blocks b with the same b // 64 in a phase, one has all 128 slots live.
All inputs are finite; a program needn't handle non-finite values.
Results may differ from a plain program's by a relative error of at most 0.0003.
Values sent between devices are 32-bit elements; how exact they have to be, the bound alone decides.
A program may use at most 64 MiB of HBM per device.

v0:
```python
import jax
import jax.numpy as jnp
from jax import lax
from jax.experimental import pallas as pl
from jax.experimental.pallas import tpu as pltpu
from jax.sharding import PartitionSpec as P

F32 = jnp.float32
BF16 = jnp.bfloat16
DT = 0.05
MESH = pl.DeviceIdType.MESH

FX, WY, WZ, MASS, QX, QY, QZ, S2 = 0, 6, 9, 12, 13, 14, 15, 16
NROW = 17


def split(value):
    high = value.astype(BF16)
    low = (value - high.astype(F32)).astype(BF16)
    return high, low


def factors(frac):
    r = frac - 0.5
    return 0.5 * (0.5 - r) * (0.5 - r), 0.75 - r * r, 0.5 * (0.5 + r) * (0.5 + r)


def kernel(
    cell_ref,
    count_ref,
    frac_in,
    vel_in,
    mass_ref,
    stress_in,
    drag_ref,
    frac_out,
    vel_out,
    stress_out,
    live_s,
    rows_s,
    base_s,
    ph_s,
    pl_s,
    fz_s,
    fzt_s,
    even_s,
    odd_s,
    vt_s,
    red_s,
    grid_s,
    edge_s,
    left_s,
    right_s,
    other_s,
    coef_s,
    send_sem,
    recv_sem,
):
    n_space = lax.axis_size("space")
    me = lax.axis_index("space")
    phase = lax.axis_index("phase")
    right = lax.rem(me + 1, n_space)
    left = lax.rem(me + n_space - 1, n_space)
    to_left = (left, phase)
    to_right = (right, phase)
    to_other = (me, 1 - phase)

    barrier = pltpu.get_barrier_semaphore()
    for target in (to_left, to_right, to_other):
        pl.semaphore_signal(barrier, inc=1, device_id=target, device_id_type=MESH)
    pl.semaphore_wait(barrier, 3)

    def remote(src, dst, sem, target):
        return pltpu.make_async_remote_copy(
            src_ref=src,
            dst_ref=dst,
            send_sem=send_sem.at[sem],
            recv_sem=recv_sem.at[sem],
            device_id=target,
            device_id_type=MESH,
        )

    coef_copies = (
        remote(drag_ref.at[0], coef_s.at[1], 0, to_left),
        remote(drag_ref.at[3], coef_s.at[0], 1, to_right),
    )
    for copy in coef_copies:
        copy.start()

    sub8 = lax.broadcasted_iota(jnp.int32, (8, 128), 0)
    zero8 = jnp.zeros((8, 128), F32)

    diagonal = lax.broadcasted_iota(jnp.int32, (64, 64), 0) == lax.broadcasted_iota(jnp.int32, (64, 64), 1)
    counts = jnp.broadcast_to(count_ref[...].astype(F32), (64, 64))
    counts = jnp.sum(jnp.where(diagonal, counts, 0.0), axis=1, keepdims=True)
    slots = lax.broadcasted_iota(jnp.int32, (64, 128), 1).astype(F32)
    live_s[...] = jnp.where(slots < counts, 1.0, 0.0)

    for c in range(5):
        even_s[c, 128:136, :] = zero8
        odd_s[c, 0:8, :] = zero8
    for c in range(4):
        vt_s[c, 0:8, :] = zero8
        vt_s[c, 136:144, :] = zero8

    def coords(j, frac):
        here = pl.ds(pl.multiple_of(8 * j, 8), 8)
        cell = cell_ref[here, :]
        cx = cell >> 4
        cy = (cell >> 2) & 3
        cz = cell & 3
        by = j // 4
        pos_x = cx.astype(F32) + (frac[0, here, :] - 2.0)
        pos_y = (cy + 4 * by).astype(F32) + (frac[1, here, :] - 4.0)
        return here, cx, cy, cz, by, pos_x, pos_y

    def prepare(frac, vel, stress):
        def body(j, carry):
            here, cx, cy, cz, by, pos_x, pos_y = coords(j, frac)
            wx = factors(frac[0, here, :])
            wy = factors(frac[1, here, :])
            wz = factors(frac[2, here, :])
            at = [cx == k for k in range(4)]
            for a in range(6):
                value = zero8
                for k in range(4):
                    if 0 <= a - k <= 2:
                        value = jnp.where(at[k], wx[a - k], value)
                rows_s[FX + a, here, :] = value
            for k in range(3):
                rows_s[WY + k, here, :] = wy[k]
                rows_s[WZ + k, here, :] = wz[k]
            base_s[0, here, :] = cy + (4 * by - 1)
            base_s[1, here, :] = (cz + 4 * (sub8 & 1) - 1) & 7
            live = live_s[here, :] > 0.5
            m = jnp.where(live, mass_ref[here, :], 0.0)
            s2 = jnp.where(live, stress[here, :], 0.0) * (4.0 * DT)
            rows_s[MASS, here, :] = m
            rows_s[S2, here, :] = s2
            rows_s[QX, here, :] = m * vel[0, here, :] - s2 * pos_x
            rows_s[QY, here, :] = m * vel[1, here, :] - s2 * pos_y
            rows_s[QZ, here, :] = m * vel[2, here, :] - s2 * (frac[2, here, :] - 0.5)
            return carry

        lax.fori_loop(0, 8, body, 0)

    def deposit():
        def body(i, carry):
            for par in range(2):
                bz = 2 * i + par
                plane = []
                column = []
                for by in range(2):
                    at = pl.ds(bz + 32 * by, 1)

                    def row(f):
                        return jnp.broadcast_to(rows_s[f, at, :], (8, 128))

                    t = sub8 - jnp.broadcast_to(base_s[0, at, :], (8, 128))
                    fy = jnp.where(t == 0, row(WY), jnp.where(t == 1, row(WY + 1), jnp.where(t == 2, row(WY + 2), 0.0)))
                    t = (sub8 - jnp.broadcast_to(base_s[1, at, :], (8, 128))) & 7
                    fz = jnp.where(t == 0, row(WZ), jnp.where(t == 1, row(WZ + 1), jnp.where(t == 2, row(WZ + 2), 0.0)))
                    tm1 = (t - 1).astype(F32)
                    s2 = row(S2)
                    plane.append(jnp.concatenate([row(FX + a) * fy for a in range(6)], axis=0))
                    column.append(
                        jnp.concatenate(
                            [
                                row(MASS) * fz,
                                row(QX) * fz,
                                row(QY) * fz,
                                (row(QZ) + s2 * tm1) * fz,
                                s2 * fz,
                            ],
                            axis=0,
                        )
                    )
                    here = pl.ds(pl.multiple_of(8 * bz, 8), 8)
                    fz_s[by, here, :] = fz
                    fzt_s[by, here, :] = fz * tm1
                plane_hi, plane_lo = split(jnp.concatenate(plane, axis=1))
                ph_s[bz] = plane_hi
                pl_s[bz] = plane_lo
                column_hi, column_lo = split(jnp.concatenate(column, axis=1))
                out = lax.dot_general(
                    jnp.concatenate([column_hi, column_lo], axis=0),
                    jnp.concatenate([plane_hi, plane_lo, jnp.zeros((32, 256), BF16)], axis=0),
                    (((1,), (1,)), ((), ())),
                    preferred_element_type=F32,
                )
                out = out[:40] + out[40:]
                for c in range(5):
                    if par == 0:
                        even_s[c, pl.ds(pl.multiple_of(8 * i, 8), 8), :] = out[8 * c : 8 * c + 8]
                    else:
                        odd_s[c, pl.ds(pl.multiple_of(8 * i + 8, 8), 8), :] = out[8 * c : 8 * c + 8]
            return carry

        lax.fori_loop(0, 16, body, 0)
        fields = []
        row7 = (lax.broadcasted_iota(jnp.int32, (128, 128), 0) & 7) == 7
        row0 = (lax.broadcasted_iota(jnp.int32, (128, 128), 0) & 7) == 0
        for c in range(5):
            total = jnp.where(row7, even_s[c, 8:136, :], even_s[c, 0:128, :]) + jnp.where(
                row0, odd_s[c, 0:128, :], odd_s[c, 8:136, :]
            )
            turned = total.T
            fields.append((turned[0:48] + turned[48:96]).reshape(6, 8, 128))
        y = lax.broadcasted_iota(jnp.int32, (8, 128), 0).astype(F32) - 3.5
        for a in range(6):
            grid_s[a, 0] = fields[0][a]
            grid_s[a, 1] = fields[1][a] + (a - 2.5) * fields[4][a]
            grid_s[a, 2] = fields[2][a] + y * fields[4][a]
            grid_s[a, 3] = fields[3][a]

    floor = lax.broadcasted_iota(jnp.int32, (8, 128), 1) == 0

    def velocity(mass, momentum):
        inverse = 1.0 / jnp.maximum(mass, 0.25)
        v = [momentum[e] * inverse for e in range(3)]
        v[2] = v[2] - DT
        v[2] = jnp.where(floor, jnp.maximum(v[2], 0.0), v[2])
        return v

    def gather(node_vel, frac, vel, stress):
        y = lax.broadcasted_iota(jnp.int32, (8, 128), 0).astype(F32) - 3.5
        for c in range(4):
            if c < 3:
                values = [node_vel[a][c] for a in range(6)]
            else:
                values = [(a - 2.5) * node_vel[a][0] + y * node_vel[a][1] for a in range(6)]
            values = jnp.concatenate(values, axis=0)
            high = values.astype(BF16).astype(F32)
            turned = jnp.concatenate([high, values - high, jnp.zeros((32, 128), F32)], axis=0).T
            vt_s[c, 8:136, :] = turned

        def body(i, carry):
            for par in range(2):
                bz = 2 * i + par
                window = []
                for c in range(4):
                    here = vt_s[c, pl.ds(pl.multiple_of(8 * i + 8, 8), 8), :]
                    if par == 0:
                        beside = vt_s[c, pl.ds(pl.multiple_of(8 * i, 8), 8), :]
                        window.append(jnp.where(sub8 == 7, beside, here))
                    else:
                        beside = vt_s[c, pl.ds(pl.multiple_of(8 * i + 16, 8), 8), :]
                        window.append(jnp.where(sub8 == 0, beside, here))
                window = jnp.concatenate(window, axis=0).astype(BF16)
                high, low, none = ph_s[bz], pl_s[bz], jnp.zeros((32, 256), BF16)
                out = jnp.dot(
                    jnp.concatenate([window, window], axis=1),
                    jnp.concatenate([high, high, none, low, low, none], axis=0),
                    preferred_element_type=F32,
                )
                at = pl.ds(pl.multiple_of(8 * bz, 8), 8)
                for by in range(2):
                    fz, fzt = fz_s[by, at, :], fzt_s[by, at, :]
                    u = [out[8 * c : 8 * c + 8, 128 * by : 128 * by + 128] for c in range(4)]
                    for c in range(3):
                        red_s[2 * c + by, at, :] = fz * u[c]
                    red_s[6 + by, at, :] = fz * u[3] + fzt * u[2]
            return carry

        lax.fori_loop(0, 16, body, 0)

        for j in range(8):
            here, cx, cy, cz, by, pos_x, pos_y = coords(j, frac)
            sums = []
            for c in range(4):
                value = red_s[2 * c + by, pl.ds(64 * (j % 4), 8, stride=8), :]
                for s in range(1, 8):
                    value = value + red_s[2 * c + by, pl.ds(64 * (j % 4) + s, 8, stride=8), :]
                sums.append(value)
            live = live_s[here, :] > 0.5
            rate = sums[3] - pos_x * sums[0] - pos_y * sums[1] - (frac[2, here, :] - 0.5) * sums[2]
            stress_out[here, :] = stress[here, :] - jnp.where(live, (4.0 * 4.0 * DT) * rate, 0.0)
            for e in range(3):
                f = frac[e, here, :]
                frac_out[e, here, :] = jnp.where(live, f + DT * sums[e], f)
                vel_out[e, here, :] = jnp.where(live, sums[e], vel[e, here, :])

    first = me == 0
    last = me == n_space - 1

    for step in range(2):
        frac, vel, stress = (frac_in, vel_in, stress_in) if step == 0 else (frac_out, vel_out, stress_out)
        prepare(frac, vel, stress)
        deposit()
        copies = [
            remote(grid_s.at[0:2], right_s.at[step], 2 + 2 * step, to_left),
            remote(grid_s.at[4:6], left_s.at[step], 3 + 2 * step, to_right),
        ]
        for copy in copies:
            copy.start()
        if step == 0:
            inner = remote(grid_s.at[2:4], other_s.at[2:4], 6, to_other)
            inner.start()
        for copy in copies:
            copy.wait()
        for a in range(2):
            for c in range(4):
                edge_s[a, c] = grid_s[a, c] + jnp.where(first, 0.0, left_s[step, a, c])
                edge_s[2 + a, c] = grid_s[4 + a, c] + jnp.where(last, 0.0, right_s[step, a, c])
        if step == 0:
            outer = [
                remote(edge_s.at[0:2], other_s.at[0:2], 7, to_other),
                remote(edge_s.at[2:4], other_s.at[4:6], 8, to_other),
            ]
            for copy in outer:
                copy.start()
        full = []
        for a in range(6):
            if a < 2:
                full.append([edge_s[a, c] for c in range(4)])
            elif a < 4:
                full.append([grid_s[a, c] for c in range(4)])
            else:
                full.append([edge_s[a - 2, c] for c in range(4)])
        node_vel = [velocity(f[0], f[1:]) for f in full]
        if step == 0:
            for copy in coef_copies + (inner,) + tuple(outer):
                copy.wait()
            for a in range(6):
                mass = full[a][0]
                other_mass = other_s[a, 0]
                other_vel = velocity(other_mass, [other_s[a, c] for c in range(1, 4)])
                coef = coef_s[0] if a == 0 else coef_s[1] if a == 5 else drag_ref[a - 1]
                slip = [other_vel[e] - node_vel[a][e] for e in range(3)]
                rate = coef * jnp.sqrt(slip[0] * slip[0] + slip[1] * slip[1] + slip[2] * slip[2] + 0.25)
                gain = rate / (1.0 + rate) * (other_mass / (mass + other_mass + 0.25))
                node_vel[a] = [node_vel[a][e] + gain * slip[e] for e in range(3)]
        node_vel[0] = [jnp.where(first, 0.0, v) for v in node_vel[0]]
        node_vel[5] = [jnp.where(last, 0.0, v) for v in node_vel[5]]
        gather(node_vel, frac, vel, stress)


def local(cell, count, frac, vel, mass, stress, drag):
    whole = pl.BlockSpec(memory_space=pltpu.VMEM)
    frac_out, vel_out, stress_out = pl.pallas_call(
        kernel,
        out_shape=(
            jax.ShapeDtypeStruct((3, 64, 128), F32),
            jax.ShapeDtypeStruct((3, 64, 128), F32),
            jax.ShapeDtypeStruct((64, 128), F32),
        ),
        in_specs=[whole] * 7,
        out_specs=(whole,) * 3,
        scratch_shapes=[
            pltpu.VMEM((64, 128), F32),
            pltpu.VMEM((NROW, 64, 128), F32),
            pltpu.VMEM((2, 64, 128), jnp.int32),
            pltpu.VMEM((32, 48, 256), BF16),
            pltpu.VMEM((32, 48, 256), BF16),
            pltpu.VMEM((2, 256, 128), F32),
            pltpu.VMEM((2, 256, 128), F32),
            pltpu.VMEM((5, 136, 128), F32),
            pltpu.VMEM((5, 136, 128), F32),
            pltpu.VMEM((4, 144, 128), F32),
            pltpu.VMEM((8, 256, 128), F32),
            pltpu.VMEM((6, 4, 8, 128), F32),
            pltpu.VMEM((4, 4, 8, 128), F32),
            pltpu.VMEM((2, 2, 4, 8, 128), F32),
            pltpu.VMEM((2, 2, 4, 8, 128), F32),
            pltpu.VMEM((6, 4, 8, 128), F32),
            pltpu.VMEM((2, 8, 128), F32),
            pltpu.SemaphoreType.DMA((9,)),
            pltpu.SemaphoreType.DMA((9,)),
        ],
        compiler_params=pltpu.CompilerParams(
            collective_id=0, has_side_effects=True, vmem_limit_bytes=32 * 1024 * 1024
        ),
    )(cell[0], count, frac[0], vel[0], mass[0], stress[0], drag)
    return frac_out[None], vel_out[None], stress_out[None]


def solution(mesh):
    in_specs = (
        P("phase", "space", None),
        P("phase", "space"),
        P("phase", None, "space", None),
        P("phase", None, "space", None),
        P("phase", "space", None),
        P("phase", "space", None),
        P("space", None, None),
    )
    out_specs = (
        P("phase", None, "space", None),
        P("phase", None, "space", None),
        P("phase", "space", None),
    )
    return jax.shard_map(local, mesh=mesh, in_specs=in_specs, out_specs=out_specs, check_vma=False)
```

profile of v0, /device:TPU:0, one launch (start us, length us, event | category | flops | bytes accessed | tf_op | source)
XLA Modules:
  0.0 44.0 jit_solution(9740223393952124071)
XLA Ops:
  0.6 0.0 copy-start.6
  0.6 0.6 %copy-done.6 = s32[1,64]{1,0:T(1,128)S(1)} copy-done((s32[1,64]{1,0:T(1,128)S(1)}, s32[1,64]{1,0:T(1,128)}, u32[]{:S(2)}) %copy-start.6) | copy-done | bytes 280
  1.3 0.0 copy-start
  1.3 0.9 %copy-done = f32[1,3,64,128]{3,2,1,0:T(8,128)S(1)} copy-done((f32[1,3,64,128]{3,2,1,0:T(8,128)S(1)}, f32[1,3,64,128]{3,2,1,0:T(8,128)}, u32[]{:S(2)}) %copy-start) | copy-done | bytes 98328
  2.2 0.0 copy-start.1
  2.2 0.9 %copy-done.1 = f32[1,3,64,128]{3,2,1,0:T(8,128)S(1)} copy-done((f32[1,3,64,128]{3,2,1,0:T(8,128)S(1)}, f32[1,3,64,128]{3,2,1,0:T(8,128)}, u32[]{:S(2)}) %copy-start.1) | copy-done | bytes 98328
  3.1 0.0 copy-start.2
  3.1 0.8 %copy-done.2 = s32[1,64,128]{2,1,0:T(8,128)S(1)} copy-done((s32[1,64,128]{2,1,0:T(8,128)S(1)}, s32[1,64,128]{2,1,0:T(8,128)}, u32[]{:S(2)}) %copy-start.2) | copy-done | bytes 32792
  3.8 0.0 copy-start.3
  3.8 0.8 %copy-done.3 = f32[1,64,128]{2,1,0:T(8,128)S(1)} copy-done((f32[1,64,128]{2,1,0:T(8,128)S(1)}, f32[1,64,128]{2,1,0:T(8,128)}, u32[]{:S(2)}) %copy-start.3) | copy-done | bytes 32792
  4.6 0.0 copy-start.4
  4.6 0.8 %copy-done.4 = f32[1,64,128]{2,1,0:T(8,128)S(1)} copy-done((f32[1,64,128]{2,1,0:T(8,128)S(1)}, f32[1,64,128]{2,1,0:T(8,128)}, u32[]{:S(2)}) %copy-start.4) | copy-done | bytes 32792
  5.4 0.0 copy-start.5
  5.4 0.7 %copy-done.5 = f32[4,8,128]{2,1,0:T(8,128)S(1)} copy-done((f32[4,8,128]{2,1,0:T(8,128)S(1)}, f32[4,8,128]{2,1,0:T(8,128)}, u32[]{:S(2)}) %copy-start.5) | copy-done | bytes 16408
  6.1 36.0 %shard_map.94 = (f32[3,64,128]{2,1,0:T(8,128)S(1)}, f32[3,64,128]{2,1,0:T(8,128)S(1)}, f32[64,128]{1,0:T(8,128)S(1)}) custom-call(s32[64,128]{1,0:T(8,128)S(1)} %bitcast.12, s32[1,64]{1,0:T(1,128)S(1)} %copy-done.6, f32[3,64,128]{2,1,0:T(8,128)S(1)} %bitcast.8, f32[3,64,128]{2,1,0:T(8,128)S(1)} %bitcast.9, f32[64,128]{1,0:T(8,128)S(1)} %bitcast.13, ...), custom_call_target="tpu_custom_call" | custom-call | tf_op jit(solution)/shard_map/pallas_call | solution.py:340
  42.1 0.6 %copy.13 = f32[1,3,64,128]{3,2,1,0:T(8,128)} copy(f32[1,3,64,128]{3,2,1,0:T(8,128)S(1)} %bitcast.11) | data formatting | bytes 196608
  42.8 0.6 %copy.14 = f32[1,3,64,128]{3,2,1,0:T(8,128)} copy(f32[1,3,64,128]{3,2,1,0:T(8,128)S(1)} %bitcast.10) | data formatting | bytes 196608
  43.4 0.6 %copy.15 = f32[1,64,128]{2,1,0:T(8,128)} copy(f32[1,64,128]{2,1,0:T(8,128)S(1)} %bitcast.15) | data formatting | bytes 65536
Async XLA Ops:
  0.6 0.7 %copy-start.6 = (s32[1,64]{1,0:T(1,128)S(1)}, s32[1,64]{1,0:T(1,128)}, u32[]{:S(2)}) copy-start(s32[1,64]{1,0:T(1,128)} %count_ref.1) | copy-start | bytes 772
  1.3 0.9 %copy-start = (f32[1,3,64,128]{3,2,1,0:T(8,128)S(1)}, f32[1,3,64,128]{3,2,1,0:T(8,128)}, u32[]{:S(2)}) copy-start(f32[1,3,64,128]{3,2,1,0:T(8,128)} %param.9) | copy-start | bytes 294916
  2.2 0.9 %copy-start.1 = (f32[1,3,64,128]{3,2,1,0:T(8,128)S(1)}, f32[1,3,64,128]{3,2,1,0:T(8,128)}, u32[]{:S(2)}) copy-start(f32[1,3,64,128]{3,2,1,0:T(8,128)} %param.10) | copy-start | bytes 294916
  3.1 0.8 %copy-start.2 = (s32[1,64,128]{2,1,0:T(8,128)S(1)}, s32[1,64,128]{2,1,0:T(8,128)}, u32[]{:S(2)}) copy-start(s32[1,64,128]{2,1,0:T(8,128)} %param.7) | copy-start | bytes 98308
  3.8 0.8 %copy-start.3 = (f32[1,64,128]{2,1,0:T(8,128)S(1)}, f32[1,64,128]{2,1,0:T(8,128)}, u32[]{:S(2)}) copy-start(f32[1,64,128]{2,1,0:T(8,128)} %param.11) | copy-start | bytes 98308
  4.6 0.8 %copy-start.4 = (f32[1,64,128]{2,1,0:T(8,128)S(1)}, f32[1,64,128]{2,1,0:T(8,128)}, u32[]{:S(2)}) copy-start(f32[1,64,128]{2,1,0:T(8,128)} %param.12) | copy-start | bytes 98308
  5.4 0.7 %copy-start.5 = (f32[4,8,128]{2,1,0:T(8,128)S(1)}, f32[4,8,128]{2,1,0:T(8,128)}, u32[]{:S(2)}) copy-start(f32[4,8,128]{2,1,0:T(8,128)} %drag_ref.1) | copy-start | bytes 49156
where the time goes:
time: 44.4 us; the launch traced here: 44 us
  Pallas kernels  36 us (81%)
  local copies, waits for them, and re-layouts  7.32 us (16%)
  between operations  0.66 us (1%)
    pallas_call x1, Pallas kernels, local(): pl.pallas_call(kernel, out_shape=(jax.ShapeDtypeStruct((3, 64, 128), F32)...  36 us
    unnamed x17, local copies, waits for them, and re-layouts  7.32 us

commit v1 on v0

v1 whole, which is shorter than its diff:
```python
import jax
import jax.numpy as jnp
from jax import lax
from jax.experimental import pallas as pl
from jax.experimental.pallas import tpu as pltpu
from jax.sharding import PartitionSpec as P

F32 = jnp.float32
BF16 = jnp.bfloat16
DT = 0.05
MESH = pl.DeviceIdType.MESH

FX, WY, WZ, MASS, QX, QY, QZ, S2 = 0, 6, 9, 12, 13, 14, 15, 16
NROW = 17


def split(value):
    high = value.astype(BF16)
    low = (value - high.astype(F32)).astype(BF16)
    return high, low


def factors(frac):
    r = frac - 0.5
    return 0.5 * (0.5 - r) * (0.5 - r), 0.75 - r * r, 0.5 * (0.5 + r) * (0.5 + r)


def coords(cell_ref, frac, j):
    here = pl.ds(8 * j, 8)
    cell = cell_ref[here, :]
    cx = cell >> 4
    cy = (cell >> 2) & 3
    cz = cell & 3
    by = j // 4
    pos_x = cx.astype(F32) + (frac[0, here, :] - 2.0)
    pos_y = (cy + 4 * by).astype(F32) + (frac[1, here, :] - 4.0)
    return here, cx, cy, cz, by, pos_x, pos_y


def gather(vt_s, ph_s, pl_s, fz_s, fzt_s, red_s, cell_ref, live_s, state, out):
    frac, vel, stress = state
    frac_out, vel_out, stress_out = out
    sub8 = lax.broadcasted_iota(jnp.int32, (8, 128), 0)

    def body(i, carry):
        for par in range(2):
            bz = 2 * i + par
            window = []
            for c in range(4):
                here = vt_s[c, pl.ds(pl.multiple_of(8 * i + 8, 8), 8), :]
                if par == 0:
                    beside = vt_s[c, pl.ds(pl.multiple_of(8 * i, 8), 8), :]
                    window.append(jnp.where(sub8 == 7, beside, here))
                else:
                    beside = vt_s[c, pl.ds(pl.multiple_of(8 * i + 16, 8), 8), :]
                    window.append(jnp.where(sub8 == 0, beside, here))
            window = jnp.concatenate(window, axis=0).astype(BF16)
            high, low, none = ph_s[bz], pl_s[bz], jnp.zeros((32, 256), BF16)
            got = jnp.dot(
                jnp.concatenate([window, window], axis=1),
                jnp.concatenate([high, high, none, low, low, none], axis=0),
                preferred_element_type=F32,
            )
            at = pl.ds(pl.multiple_of(8 * bz, 8), 8)
            for by in range(2):
                fz, fzt = fz_s[by, at, :], fzt_s[by, at, :]
                u = [got[8 * c : 8 * c + 8, 128 * by : 128 * by + 128] for c in range(4)]
                for c in range(3):
                    red_s[2 * c + by, at, :] = fz * u[c]
                red_s[6 + by, at, :] = fz * u[3] + fzt * u[2]
        return carry

    lax.fori_loop(0, 16, body, 0, unroll=16)

    for j in range(8):
        here, cx, cy, cz, by, pos_x, pos_y = coords(cell_ref, frac, j)
        sums = []
        for c in range(4):
            parts = [red_s[2 * c + by, pl.ds(64 * (j % 4) + s, 8, stride=8), :] for s in range(8)]
            while len(parts) > 1:
                parts = [parts[k] + parts[k + 1] for k in range(0, len(parts), 2)]
            sums.append(parts[0])
        live = live_s[here, :] > 0.5
        rate = sums[3] - pos_x * sums[0] - pos_y * sums[1] - (frac[2, here, :] - 0.5) * sums[2]
        stress_out[here, :] = stress[here, :] - jnp.where(live, (4.0 * 4.0 * DT) * rate, 0.0)
        for e in range(3):
            f = frac[e, here, :]
            frac_out[e, here, :] = jnp.where(live, f + DT * sums[e], f)
            vel_out[e, here, :] = jnp.where(live, sums[e], vel[e, here, :])


def nodes_kernel(
    cell_hbm,
    count_hbm,
    frac_hbm,
    vel_hbm,
    mass_hbm,
    stress_hbm,
    drag_hbm,
    cell_ref,
    live_s,
    frac_mid,
    vel_mid,
    stress_mid,
    ph_s,
    pl_s,
    fz_s,
    fzt_s,
    vt_s,
    count_ref,
    frac_in,
    vel_in,
    mass_ref,
    stress_in,
    drag_ref,
    rows_s,
    base_s,
    even_s,
    odd_s,
    red_s,
    grid_s,
    left_s,
    right_s,
    cross_left_s,
    cross_right_s,
    other_s,
    load_sem,
    send_sem,
    recv_sem,
):
    n_space = lax.axis_size("space")
    me = lax.axis_index("space")
    phase = lax.axis_index("phase")
    right = lax.rem(me + 1, n_space)
    left = lax.rem(me + n_space - 1, n_space)
    to_left = (left, phase)
    to_right = (right, phase)
    to_other = (me, 1 - phase)
    to_cross_left = (left, 1 - phase)
    to_cross_right = (right, 1 - phase)

    barrier = pltpu.get_barrier_semaphore()
    for target in (to_left, to_right, to_other, to_cross_left, to_cross_right):
        pl.semaphore_signal(barrier, inc=1, device_id=target, device_id_type=MESH)

    loads = [
        pltpu.make_async_copy(src, dst, load_sem.at[k])
        for k, (src, dst) in enumerate(
            (
                (frac_hbm, frac_in),
                (cell_hbm, cell_ref),
                (count_hbm, count_ref),
                (vel_hbm, vel_in),
                (mass_hbm, mass_ref),
                (stress_hbm, stress_in),
                (drag_hbm, drag_ref),
            )
        )
    ]
    for load in loads:
        load.start()

    def remote(src, dst, sem, target):
        return pltpu.make_async_remote_copy(
            src_ref=src,
            dst_ref=dst,
            send_sem=send_sem.at[sem],
            recv_sem=recv_sem.at[sem],
            device_id=target,
            device_id_type=MESH,
        )

    sub8 = lax.broadcasted_iota(jnp.int32, (8, 128), 0)
    zero8 = jnp.zeros((8, 128), F32)
    for c in range(5):
        even_s[c, 128:136, :] = zero8
        odd_s[c, 0:8, :] = zero8
    for c in range(4):
        vt_s[c, 0:8, :] = zero8
        vt_s[c, 136:144, :] = zero8

    for load in loads:
        load.wait()

    diagonal = lax.broadcasted_iota(jnp.int32, (64, 64), 0) == lax.broadcasted_iota(jnp.int32, (64, 64), 1)
    counts = jnp.broadcast_to(count_ref[...].astype(F32), (64, 64))
    counts = jnp.sum(jnp.where(diagonal, counts, 0.0), axis=1, keepdims=True)
    slots = lax.broadcasted_iota(jnp.int32, (64, 128), 1).astype(F32)
    live_s[...] = jnp.where(slots < counts, 1.0, 0.0)

    def prepare(frac, vel, stress):
        for j in range(8):
            here, cx, cy, cz, by, pos_x, pos_y = coords(cell_ref, frac, j)
            wx = factors(frac[0, here, :])
            wy = factors(frac[1, here, :])
            wz = factors(frac[2, here, :])
            at = [cx == k for k in range(4)]
            for a in range(6):
                value = zero8
                for k in range(4):
                    if 0 <= a - k <= 2:
                        value = jnp.where(at[k], wx[a - k], value)
                rows_s[FX + a, here, :] = value
            for k in range(3):
                rows_s[WY + k, here, :] = wy[k]
                rows_s[WZ + k, here, :] = wz[k]
            base_s[0, here, :] = cy + (4 * by - 1)
            base_s[1, here, :] = (cz + 4 * (sub8 & 1) - 1) & 7
            live = live_s[here, :] > 0.5
            m = jnp.where(live, mass_ref[here, :], 0.0)
            s2 = jnp.where(live, stress[here, :], 0.0) * (4.0 * DT)
            rows_s[MASS, here, :] = m
            rows_s[S2, here, :] = s2
            rows_s[QX, here, :] = m * vel[0, here, :] - s2 * pos_x
            rows_s[QY, here, :] = m * vel[1, here, :] - s2 * pos_y
            rows_s[QZ, here, :] = m * vel[2, here, :] - s2 * (frac[2, here, :] - 0.5)

    def deposit(step):
        def body(i, carry):
            for par in range(2):
                bz = 2 * i + par
                plane = []
                column = []
                for by in range(2):
                    at = pl.ds(bz + 32 * by, 1)

                    def row(f):
                        return jnp.broadcast_to(rows_s[f, at, :], (8, 128))

                    t = sub8 - jnp.broadcast_to(base_s[0, at, :], (8, 128))
                    fy = jnp.where(t == 0, row(WY), jnp.where(t == 1, row(WY + 1), jnp.where(t == 2, row(WY + 2), 0.0)))
                    t = (sub8 - jnp.broadcast_to(base_s[1, at, :], (8, 128))) & 7
                    fz = jnp.where(t == 0, row(WZ), jnp.where(t == 1, row(WZ + 1), jnp.where(t == 2, row(WZ + 2), 0.0)))
                    tm1 = (t - 1).astype(F32)
                    s2 = row(S2)
                    plane.append(jnp.concatenate([row(FX + a) * fy for a in range(6)], axis=0))
                    column.append(
                        jnp.concatenate(
                            [
                                row(MASS) * fz,
                                row(QX) * fz,
                                row(QY) * fz,
                                (row(QZ) + s2 * tm1) * fz,
                                s2 * fz,
                            ],
                            axis=0,
                        )
                    )
                    here = pl.ds(pl.multiple_of(8 * bz, 8), 8)
                    fz_s[by, here, :] = fz
                    fzt_s[by, here, :] = fz * tm1
                plane_hi, plane_lo = split(jnp.concatenate(plane, axis=1))
                ph_s[bz] = plane_hi
                pl_s[bz] = plane_lo
                column_hi, column_lo = split(jnp.concatenate(column, axis=1))
                out = lax.dot_general(
                    jnp.concatenate([column_hi, column_lo], axis=0),
                    jnp.concatenate([plane_hi, plane_lo, jnp.zeros((32, 256), BF16)], axis=0),
                    (((1,), (1,)), ((), ())),
                    preferred_element_type=F32,
                )
                out = out[:40] + out[40:]
                for c in range(5):
                    if par == 0:
                        even_s[c, pl.ds(pl.multiple_of(8 * i, 8), 8), :] = out[8 * c : 8 * c + 8]
                    else:
                        odd_s[c, pl.ds(pl.multiple_of(8 * i + 8, 8), 8), :] = out[8 * c : 8 * c + 8]
            return carry

        lax.fori_loop(0, 16, body, 0, unroll=16)
        fields = []
        row7 = (lax.broadcasted_iota(jnp.int32, (128, 128), 0) & 7) == 7
        row0 = (lax.broadcasted_iota(jnp.int32, (128, 128), 0) & 7) == 0
        for c in range(5):
            total = jnp.where(row7, even_s[c, 8:136, :], even_s[c, 0:128, :]) + jnp.where(
                row0, odd_s[c, 0:128, :], odd_s[c, 8:136, :]
            )
            turned = total.T
            fields.append((turned[0:48] + turned[48:96]).reshape(6, 8, 128))
        y = sub8.astype(F32) - 3.5
        for a in range(6):
            grid_s[step, a, 0] = fields[0][a]
            grid_s[step, a, 1] = fields[1][a] + (a - 2.5) * fields[4][a]
            grid_s[step, a, 2] = fields[2][a] + y * fields[4][a]
            grid_s[step, a, 3] = fields[3][a]

    floor = lax.broadcasted_iota(jnp.int32, (8, 128), 1) == 0

    def velocity(mass, momentum):
        inverse = 1.0 / jnp.maximum(mass, 0.25)
        v = [momentum[e] * inverse for e in range(3)]
        v[2] = v[2] - DT
        v[2] = jnp.where(floor, jnp.maximum(v[2], 0.0), v[2])
        return v

    def turn(node_vel):
        y = sub8.astype(F32) - 3.5
        for c in range(4):
            if c < 3:
                values = [node_vel[a][c] for a in range(6)]
            else:
                values = [(a - 2.5) * node_vel[a][0] + y * node_vel[a][1] for a in range(6)]
            values = jnp.concatenate(values, axis=0)
            high = values.astype(BF16).astype(F32)
            turned = jnp.concatenate([high, values - high, jnp.zeros((32, 128), F32)], axis=0).T
            vt_s[c, 8:136, :] = turned

    first = me == 0
    last = me == n_space - 1
    started = []

    def settled(a, c, mine, from_left, from_right):
        if a < 2:
            return mine[a, c] + jnp.where(first, 0.0, from_left[a, c])
        if a < 4:
            return mine[a, c]
        return mine[a, c] + jnp.where(last, 0.0, from_right[a - 4, c])

    for step in range(2):
        state = (frac_in, vel_in, stress_in) if step == 0 else (frac_mid, vel_mid, stress_mid)
        prepare(*state)
        deposit(step)
        mine = grid_s.at[step]
        if step == 0:
            for a in range(1, 5):
                mine[a, 4] = drag_ref[a - 1]
            mine[0, 4] = zero8
            mine[5, 4] = zero8
            pl.semaphore_wait(barrier, 5)
            copies = [
                remote(mine.at[0:2], right_s.at[step], 0, to_left),
                remote(mine.at[4:6], left_s.at[step], 1, to_right),
                remote(mine.at[0:2, 0:4], cross_right_s, 2, to_cross_left),
                remote(mine.at[4:6, 0:4], cross_left_s, 3, to_cross_right),
                remote(mine.at[:, 0:4], other_s, 4, to_other),
            ]
        else:
            copies = [
                remote(mine.at[0:2, 0:4], right_s.at[step, :, 0:4], 5, to_left),
                remote(mine.at[4:6, 0:4], left_s.at[step, :, 0:4], 6, to_right),
            ]
        for copy in copies:
            copy.start()
        for copy in copies:
            copy.wait_recv()
        started += copies
        node_vel = []
        for a in range(6):
            full = [settled(a, c, mine, left_s.at[step], right_s.at[step]) for c in range(4)]
            v = velocity(full[0], full[1:])
            if step == 0:
                other = [settled(a, c, other_s, cross_left_s, cross_right_s) for c in range(4)]
                other_vel = velocity(other[0], other[1:])
                coef = left_s[0, 0, 4] if a == 0 else right_s[0, 1, 4] if a == 5 else drag_ref[a - 1]
                slip = [other_vel[e] - v[e] for e in range(3)]
                rate = coef * jnp.sqrt(slip[0] * slip[0] + slip[1] * slip[1] + slip[2] * slip[2] + 0.25)
                gain = rate / (1.0 + rate) * (other[0] / (full[0] + other[0] + 0.25))
                v = [v[e] + gain * slip[e] for e in range(3)]
            if a == 0:
                v = [jnp.where(first, 0.0, value) for value in v]
            if a == 5:
                v = [jnp.where(last, 0.0, value) for value in v]
            node_vel.append(v)
        turn(node_vel)
        if step == 0:
            gather(
                vt_s, ph_s, pl_s, fz_s, fzt_s, red_s, cell_ref, live_s, state, (frac_mid, vel_mid, stress_mid)
            )
    for copy in started:
        copy.wait_send()


def particles_kernel(
    cell_ref,
    live_s,
    frac_mid,
    vel_mid,
    stress_mid,
    ph_s,
    pl_s,
    fz_s,
    fzt_s,
    vt_s,
    frac_hbm,
    vel_hbm,
    stress_hbm,
    frac_out,
    vel_out,
    stress_out,
    red_s,
    store_sem,
):
    gather(
        vt_s,
        ph_s,
        pl_s,
        fz_s,
        fzt_s,
        red_s,
        cell_ref,
        live_s,
        (frac_mid, vel_mid, stress_mid),
        (frac_out, vel_out, stress_out),
    )
    stores = [
        pltpu.make_async_copy(src, dst, store_sem.at[k])
        for k, (src, dst) in enumerate(((frac_out, frac_hbm), (vel_out, vel_hbm), (stress_out, stress_hbm)))
    ]
    for store in stores:
        store.start()
    for store in stores:
        store.wait()


def local(cell, count, frac, vel, mass, stress, drag):
    vmem = pl.BlockSpec(memory_space=pltpu.VMEM)
    anywhere = pl.BlockSpec(memory_space=pl.ANY)
    passed = [
        ((64, 128), jnp.int32),
        ((64, 128), F32),
        ((3, 64, 128), F32),
        ((3, 64, 128), F32),
        ((64, 128), F32),
        ((32, 48, 256), BF16),
        ((32, 48, 256), BF16),
        ((2, 256, 128), F32),
        ((2, 256, 128), F32),
        ((4, 144, 128), F32),
    ]
    state = pl.pallas_call(
        nodes_kernel,
        out_shape=[jax.ShapeDtypeStruct(shape, kind) for shape, kind in passed],
        in_specs=[anywhere] * 7,
        out_specs=[vmem] * len(passed),
        scratch_shapes=[
            pltpu.VMEM((1, 64), jnp.int32),
            pltpu.VMEM((3, 64, 128), F32),
            pltpu.VMEM((3, 64, 128), F32),
            pltpu.VMEM((64, 128), F32),
            pltpu.VMEM((64, 128), F32),
            pltpu.VMEM((4, 8, 128), F32),
            pltpu.VMEM((NROW, 64, 128), F32),
            pltpu.VMEM((2, 64, 128), jnp.int32),
            pltpu.VMEM((5, 136, 128), F32),
            pltpu.VMEM((5, 136, 128), F32),
            pltpu.VMEM((8, 256, 128), F32),
            pltpu.VMEM((2, 6, 5, 8, 128), F32),
            pltpu.VMEM((2, 2, 5, 8, 128), F32),
            pltpu.VMEM((2, 2, 5, 8, 128), F32),
            pltpu.VMEM((2, 4, 8, 128), F32),
            pltpu.VMEM((2, 4, 8, 128), F32),
            pltpu.VMEM((6, 4, 8, 128), F32),
            pltpu.SemaphoreType.DMA((7,)),
            pltpu.SemaphoreType.DMA((7,)),
            pltpu.SemaphoreType.DMA((7,)),
        ],
        compiler_params=pltpu.CompilerParams(
            collective_id=0, has_side_effects=True, vmem_limit_bytes=24 * 1024 * 1024
        ),
    )(*[pltpu.with_memory_space_constraint(x, pltpu.HBM) for x in (cell[0], count, frac[0], vel[0], mass[0], stress[0], drag)])
    frac_out, vel_out, stress_out = pl.pallas_call(
        particles_kernel,
        out_shape=[
            jax.ShapeDtypeStruct((3, 64, 128), F32),
            jax.ShapeDtypeStruct((3, 64, 128), F32),
            jax.ShapeDtypeStruct((64, 128), F32),
        ],
        in_specs=[vmem] * len(passed),
        out_specs=[anywhere] * 3,
        scratch_shapes=[
            pltpu.VMEM((3, 64, 128), F32),
            pltpu.VMEM((3, 64, 128), F32),
            pltpu.VMEM((64, 128), F32),
            pltpu.VMEM((8, 256, 128), F32),
            pltpu.SemaphoreType.DMA((3,)),
        ],
        compiler_params=pltpu.CompilerParams(vmem_limit_bytes=24 * 1024 * 1024),
    )(*state)
    return frac_out[None], vel_out[None], stress_out[None]


def solution(mesh):
    in_specs = (
        P("phase", "space", None),
        P("phase", "space"),
        P("phase", None, "space", None),
        P("phase", None, "space", None),
        P("phase", "space", None),
        P("phase", "space", None),
        P("space", None, None),
    )
    out_specs = (
        P("phase", None, "space", None),
        P("phase", None, "space", None),
        P("phase", "space", None),
    )
    return jax.shard_map(local, mesh=mesh, in_specs=in_specs, out_specs=out_specs, check_vma=False)
```

time: 44.4 us -> 27.2 us (0.61)
  the two profiles are of different devices: /device:TPU:0 before, /device:TPU:24 now
where the time goes in v1:
time: 27.2 us; the launch traced here: 26.8 us
  Pallas kernels  26.1 us (96%)
  between operations  0.64 us (2%)
    pallas_call x1, Pallas kernels, local(): pl.pallas_call(nodes_kernel, out_shape=[jax.ShapeDtypeStruct(shape, kind)...  24.6 us
    pallas_call x1, Pallas kernels, local(): pl.pallas_call(particles_kernel, out_shape=[jax.ShapeDtypeStruct((3, 64,...  1.53 us

profile of v1, /device:TPU:24, one launch (start us, length us, event | category | flops | bytes accessed | tf_op | source)
XLA Modules:
  0.0 26.8 jit_solution(5283663305939883906)
XLA Ops:
  0.6 24.6 %shard_map.94 = (s32[64,128]{1,0:T(8,128)S(1)}, f32[64,128]{1,0:T(8,128)S(1)}, f32[3,64,128]{2,1,0:T(8,128)S(1)}, f32[3,64,128]{2,1,0:T(8,128)S(1)}, f32[64,128]...) custom-call(s32[64,128]{1,0:T(8,128)} %bitcast.10, ...), custom_call_target="tpu_custom_call" | custom-call | tf_op jit(solution)/shard_map/pallas_call | solution.py:430
  25.2 1.5 %shard_map.95 = (f32[3,64,128]{2,1,0:T(8,128)}, f32[3,64,128]{2,1,0:T(8,128)}, f32[64,128]{1,0:T(8,128)}) custom-call(s32[64,128]{1,0:T(8,128)S(1)} %get-tuple-element.16.cell_ref, f32[64,128]{1,0:T(8,128)S(1)} %get-tuple-element.17.live_s, f32[3,64,128]{2,1,0:T(8,128)S(1)} %get-tuple-element.18.frac_mid, f32[3,64,128]{2,1,0:T(8,128)S(1)} %get-tuple-element.19.vel_mid, ...), custom_call_target="tpu_custom_call" | custom-call | tf_op jit(solution)/shard_map/pallas_call | solution.py:461

commit v2 on v1

--- a/solution.py
+++ b/solution.py
@@ -9,6 +9,7 @@
 BF16 = jnp.bfloat16
 DT = 0.05
 MESH = pl.DeviceIdType.MESH
+RUN = 32
 
 FX, WY, WZ, MASS, QX, QY, QZ, S2 = 0, 6, 9, 12, 13, 14, 15, 16
 NROW = 17
@@ -119,6 +120,7 @@
     odd_s,
     red_s,
     grid_s,
+    edge_s,
     left_s,
     right_s,
     cross_left_s,
@@ -139,9 +141,23 @@
     to_cross_left = (left, 1 - phase)
     to_cross_right = (right, 1 - phase)
 
+    has_left = me > 0
+    has_right = me < n_space - 1
+    run_left = lax.rem(me, RUN) == 0
+    run_right = lax.rem(me, RUN) == RUN - 1
+    cross_left = jnp.logical_and(has_left, run_left)
+    cross_right = jnp.logical_and(has_right, run_right)
     barrier = pltpu.get_barrier_semaphore()
-    for target in (to_left, to_right, to_other, to_cross_left, to_cross_right):
+
+    def greet(target):
         pl.semaphore_signal(barrier, inc=1, device_id=target, device_id_type=MESH)
+
+    greet(to_other)
+    pl.when(has_left)(lambda: greet(to_left))
+    pl.when(has_right)(lambda: greet(to_right))
+    pl.when(cross_left)(lambda: greet(to_cross_left))
+    pl.when(cross_right)(lambda: greet(to_cross_right))
+    greeted = 1 + sum(flag.astype(jnp.int32) for flag in (has_left, has_right, cross_left, cross_right))
 
     loads = [
         pltpu.make_async_copy(src, dst, load_sem.at[k])
@@ -305,51 +321,84 @@
             turned = jnp.concatenate([high, values - high, jnp.zeros((32, 128), F32)], axis=0).T
             vt_s[c, 8:136, :] = turned
 
-    first = me == 0
-    last = me == n_space - 1
-    started = []
-
-    def settled(a, c, mine, from_left, from_right):
+    def settled(a, c, mine, from_left, from_right, use_left, use_right):
         if a < 2:
-            return mine[a, c] + jnp.where(first, 0.0, from_left[a, c])
+            return mine[a, c] + jnp.where(use_left, from_left[a, c], 0.0)
         if a < 4:
             return mine[a, c]
-        return mine[a, c] + jnp.where(last, 0.0, from_right[a - 4, c])
-
+        return mine[a, c] + jnp.where(use_right, from_right[a - 4, c], 0.0)
+
+    started = []
     for step in range(2):
         state = (frac_in, vel_in, stress_in) if step == 0 else (frac_mid, vel_mid, stress_mid)
         prepare(*state)
         deposit(step)
         mine = grid_s.at[step]
+        width = 5 if step == 0 else 4
+        leftward = remote(mine.at[0:2, 0:width], right_s.at[step, :, 0:width], 2 * step, to_left)
+        rightward = remote(mine.at[4:6, 0:width], left_s.at[step, :, 0:width], 2 * step + 1, to_right)
+        started += [(has_left, leftward), (has_right, rightward)]
         if step == 0:
             for a in range(1, 5):
                 mine[a, 4] = drag_ref[a - 1]
             mine[0, 4] = zero8
             mine[5, 4] = zero8
-            pl.semaphore_wait(barrier, 5)
-            copies = [
-                remote(mine.at[0:2], right_s.at[step], 0, to_left),
-                remote(mine.at[4:6], left_s.at[step], 1, to_right),
-                remote(mine.at[0:2, 0:4], cross_right_s, 2, to_cross_left),
-                remote(mine.at[4:6, 0:4], cross_left_s, 3, to_cross_right),
-                remote(mine.at[:, 0:4], other_s, 4, to_other),
-            ]
+            pl.semaphore_wait(barrier, greeted)
+        pl.when(has_left)(leftward.start)
+        pl.when(has_right)(rightward.start)
+        if step == 0:
+            inner = remote(mine.at[2:4, 0:4], other_s.at[2:4], 4, to_other)
+            inner.start()
+            cross_leftward = remote(mine.at[0:2, 0:4], cross_right_s, 5, to_cross_left)
+            cross_rightward = remote(mine.at[4:6, 0:4], cross_left_s, 6, to_cross_right)
+            raw_left = remote(mine.at[0:2, 0:4], other_s.at[0:2], 7, to_other)
+            raw_right = remote(mine.at[4:6, 0:4], other_s.at[4:6], 8, to_other)
+            sum_left = remote(edge_s.at[0:2], other_s.at[0:2], 7, to_other)
+            sum_right = remote(edge_s.at[2:4], other_s.at[4:6], 8, to_other)
+
+            def send_raw(flag, run, cross, raw):
+                pl.when(flag)(cross.start)
+                pl.when(run)(raw.start)
+
+            send_raw(cross_left, run_left, cross_leftward, raw_left)
+            send_raw(cross_right, run_right, cross_rightward, raw_right)
+            started += [(cross_left, cross_leftward), (cross_right, cross_rightward)]
+            started += [(None, inner), (None, sum_left), (None, sum_right)]
+
+            def send_sum_left():
+                rightward.wait_recv()
+                for a in range(2):
+                    for c in range(4):
+                        edge_s[a, c] = mine[a, c] + left_s[0, a, c]
+                sum_left.start()
+
+            def send_sum_right():
+                leftward.wait_recv()
+                for a in range(2):
+                    for c in range(4):
+                        edge_s[2 + a, c] = mine[4 + a, c] + right_s[0, a, c]
+                sum_right.start()
+
+            near_left = lax.rem(me, 2) == 1
+            pl.when(near_left)(send_sum_left)
+            pl.when(jnp.logical_not(run_right))(send_sum_right)
+            pl.when(jnp.logical_not(jnp.logical_or(near_left, run_left)))(send_sum_left)
+            pl.when(cross_left)(rightward.wait_recv)
+            pl.when(cross_right)(leftward.wait_recv)
+            inner.wait_recv()
+            pl.when(cross_left)(cross_rightward.wait_recv)
+            pl.when(cross_right)(cross_leftward.wait_recv)
+            sum_left.wait_recv()
+            sum_right.wait_recv()
         else:
-            copies = [
-                remote(mine.at[0:2, 0:4], right_s.at[step, :, 0:4], 5, to_left),
-                remote(mine.at[4:6, 0:4], left_s.at[step, :, 0:4], 6, to_right),
-            ]
-        for copy in copies:
-            copy.start()
-        for copy in copies:
-            copy.wait_recv()
-        started += copies
+            pl.when(has_left)(rightward.wait_recv)
+            pl.when(has_right)(leftward.wait_recv)
         node_vel = []
         for a in range(6):
-            full = [settled(a, c, mine, left_s.at[step], right_s.at[step]) for c in range(4)]
+            full = [settled(a, c, mine, left_s.at[step], right_s.at[step], has_left, has_right) for c in range(4)]
             v = velocity(full[0], full[1:])
             if step == 0:
-                other = [settled(a, c, other_s, cross_left_s, cross_right_s) for c in range(4)]
+                other = [settled(a, c, other_s, cross_left_s, cross_right_s, cross_left, cross_right) for c in range(4)]
                 other_vel = velocity(other[0], other[1:])
                 coef = left_s[0, 0, 4] if a == 0 else right_s[0, 1, 4] if a == 5 else drag_ref[a - 1]
                 slip = [other_vel[e] - v[e] for e in range(3)]
@@ -357,17 +406,20 @@
                 gain = rate / (1.0 + rate) * (other[0] / (full[0] + other[0] + 0.25))
                 v = [v[e] + gain * slip[e] for e in range(3)]
             if a == 0:
-                v = [jnp.where(first, 0.0, value) for value in v]
+                v = [jnp.where(has_left, value, 0.0) for value in v]
             if a == 5:
-                v = [jnp.where(last, 0.0, value) for value in v]
+                v = [jnp.where(has_right, value, 0.0) for value in v]
             node_vel.append(v)
         turn(node_vel)
         if step == 0:
             gather(
                 vt_s, ph_s, pl_s, fz_s, fzt_s, red_s, cell_ref, live_s, state, (frac_mid, vel_mid, stress_mid)
             )
-    for copy in started:
-        copy.wait_send()
+    for flag, copy in started:
+        if flag is None:
+            copy.wait_send()
+        else:
+            pl.when(flag)(copy.wait_send)
 
 
 def particles_kernel(
@@ -445,14 +497,15 @@
             pltpu.VMEM((5, 136, 128), F32),
             pltpu.VMEM((8, 256, 128), F32),
             pltpu.VMEM((2, 6, 5, 8, 128), F32),
+            pltpu.VMEM((4, 4, 8, 128), F32),
             pltpu.VMEM((2, 2, 5, 8, 128), F32),
             pltpu.VMEM((2, 2, 5, 8, 128), F32),
             pltpu.VMEM((2, 4, 8, 128), F32),
             pltpu.VMEM((2, 4, 8, 128), F32),
             pltpu.VMEM((6, 4, 8, 128), F32),
             pltpu.SemaphoreType.DMA((7,)),
-            pltpu.SemaphoreType.DMA((7,)),
-            pltpu.SemaphoreType.DMA((7,)),
+            pltpu.SemaphoreType.DMA((9,)),
+            pltpu.SemaphoreType.DMA((9,)),
         ],
         compiler_params=pltpu.CompilerParams(
             collective_id=0, has_side_effects=True, vmem_limit_bytes=24 * 1024 * 1024

time: 27.2 us -> 24.4 us (0.90); the launches traced: 26.8 us -> 24.3 us
  Pallas kernels: 26.1 us -> 23.7 us
    pallas_call x1, Pallas kernels: 24.6 us -> 22.1 us  [local(): pl.pallas_call(nodes_kernel, out_shape=[jax.ShapeDtypeStruct(shape, kind)...]
where the time goes in v2:
time: 24.4 us; the launch traced here: 24.3 us
  Pallas kernels  23.7 us (97%)
  between operations  0.64 us (3%)
    pallas_call x1, Pallas kernels, local(): pl.pallas_call(nodes_kernel, out_shape=[jax.ShapeDtypeStruct(shape, kind)...  22.1 us
    pallas_call x1, Pallas kernels, local(): pl.pallas_call(particles_kernel, out_shape=[jax.ShapeDtypeStruct((3, 64,...  1.54 us

profile of v2, /device:TPU:24, one launch (start us, length us, event | category | flops | bytes accessed | tf_op | source)
XLA Modules:
  0.0 24.3 jit_solution(5495678344747452450)
XLA Ops:
  0.6 22.1 %shard_map.94 = (s32[64,128]{1,0:T(8,128)S(1)}, f32[64,128]{1,0:T(8,128)S(1)}, f32[3,64,128]{2,1,0:T(8,128)S(1)}, f32[3,64,128]{2,1,0:T(8,128)S(1)}, f32[64,128]...) custom-call(s32[64,128]{1,0:T(8,128)} %bitcast.10, ...), custom_call_target="tpu_custom_call" | custom-call | tf_op jit(solution)/shard_map/pallas_call | solution.py:482
  22.8 1.5 %shard_map.95 = (f32[3,64,128]{2,1,0:T(8,128)}, f32[3,64,128]{2,1,0:T(8,128)}, f32[64,128]{1,0:T(8,128)}) custom-call(s32[64,128]{1,0:T(8,128)S(1)} %get-tuple-element.16.cell_ref, f32[64,128]{1,0:T(8,128)S(1)} %get-tuple-element.17.live_s, f32[3,64,128]{2,1,0:T(8,128)S(1)} %get-tuple-element.18.frac_mid, f32[3,64,128]{2,1,0:T(8,128)S(1)} %get-tuple-element.19.vel_mid, ...), custom_call_target="tpu_custom_call" | custom-call | tf_op jit(solution)/shard_map/pallas_call | solution.py:514

commit v3 on v2

--- a/solution.py
+++ b/solution.py
@@ -11,8 +11,8 @@
 MESH = pl.DeviceIdType.MESH
 RUN = 32
 
-FX, WY, WZ, MASS, QX, QY, QZ, S2 = 0, 6, 9, 12, 13, 14, 15, 16
-NROW = 17
+FX, MASS, QX, QY, QZ, S2 = 0, 6, 7, 8, 9, 10
+NROW = 11
 
 
 def split(value):
@@ -115,7 +115,7 @@
     stress_in,
     drag_ref,
     rows_s,
-    base_s,
+    fy_s,
     even_s,
     odd_s,
     red_s,
@@ -147,17 +147,21 @@
     run_right = lax.rem(me, RUN) == RUN - 1
     cross_left = jnp.logical_and(has_left, run_left)
     cross_right = jnp.logical_and(has_right, run_right)
+    relay_left = jnp.logical_and(cross_left, phase == 0)
+    relay_right = jnp.logical_and(cross_right, phase == 0)
+    direct_left = jnp.logical_and(has_left, jnp.logical_not(jnp.logical_and(run_left, phase == 1)))
+    direct_right = jnp.logical_and(has_right, jnp.logical_not(jnp.logical_and(run_right, phase == 1)))
     barrier = pltpu.get_barrier_semaphore()
 
     def greet(target):
         pl.semaphore_signal(barrier, inc=1, device_id=target, device_id_type=MESH)
 
     greet(to_other)
-    pl.when(has_left)(lambda: greet(to_left))
-    pl.when(has_right)(lambda: greet(to_right))
+    pl.when(direct_left)(lambda: greet(to_left))
+    pl.when(direct_right)(lambda: greet(to_right))
     pl.when(cross_left)(lambda: greet(to_cross_left))
     pl.when(cross_right)(lambda: greet(to_cross_right))
-    greeted = 1 + sum(flag.astype(jnp.int32) for flag in (has_left, has_right, cross_left, cross_right))
+    greeted = 1 + sum(flag.astype(jnp.int32) for flag in (direct_left, direct_right, cross_left, cross_right))
 
     loads = [
         pltpu.make_async_copy(src, dst, load_sem.at[k])
@@ -176,12 +180,12 @@
     for load in loads:
         load.start()
 
-    def remote(src, dst, sem, target):
+    def remote(src, dst, sem, target, arrival=None):
         return pltpu.make_async_remote_copy(
             src_ref=src,
             dst_ref=dst,
             send_sem=send_sem.at[sem],
-            recv_sem=recv_sem.at[sem],
+            recv_sem=recv_sem.at[sem if arrival is None else arrival],
             device_id=target,
             device_id_type=MESH,
         )
@@ -191,6 +195,7 @@
     for c in range(5):
         even_s[c, 128:136, :] = zero8
         odd_s[c, 0:8, :] = zero8
+    fy_s[...] = jnp.zeros((2, 256, 128), F32)
     for c in range(4):
         vt_s[c, 0:8, :] = zero8
         vt_s[c, 136:144, :] = zero8
@@ -210,18 +215,30 @@
             wx = factors(frac[0, here, :])
             wy = factors(frac[1, here, :])
             wz = factors(frac[2, here, :])
-            at = [cx == k for k in range(4)]
-            for a in range(6):
+            on_x = [cx == k for k in range(4)]
+            on_y = [cy == k for k in range(4)]
+            on_z = [cz == k for k in range(4)]
+
+            def place(on, w, node):
                 value = zero8
                 for k in range(4):
-                    if 0 <= a - k <= 2:
-                        value = jnp.where(at[k], wx[a - k], value)
-                rows_s[FX + a, here, :] = value
-            for k in range(3):
-                rows_s[WY + k, here, :] = wy[k]
-                rows_s[WZ + k, here, :] = wz[k]
-            base_s[0, here, :] = cy + (4 * by - 1)
-            base_s[1, here, :] = (cz + 4 * (sub8 & 1) - 1) & 7
+                    if 0 <= node - k <= 2 and w[node - k] is not None:
+                        value = jnp.where(on[k], w[node - k], value)
+                return value
+
+            for a in range(6):
+                rows_s[FX + a, here, :] = place(on_x, wx, a)
+            start = 64 * (j % 4)
+            for node in range(6):
+                y = 4 * by + node - 1
+                if 0 <= y < 8:
+                    fy_s[by, pl.ds(start + y, 8, stride=8), :] = place(on_y, wy, node)
+            tz = (-wz[0], None, wz[2])
+            for ref, w in ((fz_s, wz), (fzt_s, tz)):
+                nodes = [place(on_z, w, node) for node in range(6)] + [zero8, zero8]
+                for r in range(8):
+                    value = jnp.where((sub8 & 1) == 0, nodes[(r + 1) % 8], nodes[(r + 5) % 8])
+                    ref[by, pl.ds(start + r, 8, stride=8), :] = value
             live = live_s[here, :] > 0.5
             m = jnp.where(live, mass_ref[here, :], 0.0)
             s2 = jnp.where(live, stress[here, :], 0.0) * (4.0 * DT)
@@ -243,11 +260,9 @@
                     def row(f):
                         return jnp.broadcast_to(rows_s[f, at, :], (8, 128))
 
-                    t = sub8 - jnp.broadcast_to(base_s[0, at, :], (8, 128))
-                    fy = jnp.where(t == 0, row(WY), jnp.where(t == 1, row(WY + 1), jnp.where(t == 2, row(WY + 2), 0.0)))
-                    t = (sub8 - jnp.broadcast_to(base_s[1, at, :], (8, 128))) & 7
-                    fz = jnp.where(t == 0, row(WZ), jnp.where(t == 1, row(WZ + 1), jnp.where(t == 2, row(WZ + 2), 0.0)))
-                    tm1 = (t - 1).astype(F32)
+                    here = pl.ds(pl.multiple_of(8 * bz, 8), 8)
+                    fy = fy_s[by, here, :]
+                    fz = fz_s[by, here, :]
                     s2 = row(S2)
                     plane.append(jnp.concatenate([row(FX + a) * fy for a in range(6)], axis=0))
                     column.append(
@@ -256,15 +271,12 @@
                                 row(MASS) * fz,
                                 row(QX) * fz,
                                 row(QY) * fz,
-                                (row(QZ) + s2 * tm1) * fz,
+                                row(QZ) * fz + s2 * fzt_s[by, here, :],
                                 s2 * fz,
                             ],
                             axis=0,
                         )
                     )
-                    here = pl.ds(pl.multiple_of(8 * bz, 8), 8)
-                    fz_s[by, here, :] = fz
-                    fzt_s[by, here, :] = fz * tm1
                 plane_hi, plane_lo = split(jnp.concatenate(plane, axis=1))
                 ph_s[bz] = plane_hi
                 pl_s[bz] = plane_lo
@@ -329,6 +341,12 @@
         return mine[a, c] + jnp.where(use_right, from_right[a - 4, c], 0.0)
 
     started = []
+
+    def own(a, step):
+        mine = grid_s.at[step]
+        full = [settled(a, c, mine, left_s.at[step], right_s.at[step], has_left, has_right) for c in range(4)]
+        return full[0], velocity(full[0], full[1:])
+
     for step in range(2):
         state = (frac_in, vel_in, stress_in) if step == 0 else (frac_mid, vel_mid, stress_mid)
         prepare(*state)
@@ -337,20 +355,23 @@
         width = 5 if step == 0 else 4
         leftward = remote(mine.at[0:2, 0:width], right_s.at[step, :, 0:width], 2 * step, to_left)
         rightward = remote(mine.at[4:6, 0:width], left_s.at[step, :, 0:width], 2 * step + 1, to_right)
-        started += [(has_left, leftward), (has_right, rightward)]
+        go_left, go_right = (direct_left, direct_right) if step == 0 else (has_left, has_right)
+        started += [(go_left, leftward), (go_right, rightward)]
         if step == 0:
             for a in range(1, 5):
                 mine[a, 4] = drag_ref[a - 1]
             mine[0, 4] = zero8
             mine[5, 4] = zero8
             pl.semaphore_wait(barrier, greeted)
-        pl.when(has_left)(leftward.start)
-        pl.when(has_right)(rightward.start)
         if step == 0:
             inner = remote(mine.at[2:4, 0:4], other_s.at[2:4], 4, to_other)
             inner.start()
-            cross_leftward = remote(mine.at[0:2, 0:4], cross_right_s, 5, to_cross_left)
-            cross_rightward = remote(mine.at[4:6, 0:4], cross_left_s, 6, to_cross_right)
+        pl.when(go_left)(leftward.start)
+        pl.when(go_right)(rightward.start)
+        node = {a: own(a, step) for a in (2, 3)}
+        if step == 0:
+            cross_leftward = remote(mine.at[0:2], cross_right_s, 5, to_cross_left)
+            cross_rightward = remote(mine.at[4:6], cross_left_s, 6, to_cross_right)
             raw_left = remote(mine.at[0:2, 0:4], other_s.at[0:2], 7, to_other)
             raw_right = remote(mine.at[4:6, 0:4], other_s.at[4:6], 8, to_other)
             sum_left = remote(edge_s.at[0:2], other_s.at[0:2], 7, to_other)
@@ -383,27 +404,40 @@
             pl.when(near_left)(send_sum_left)
             pl.when(jnp.logical_not(run_right))(send_sum_right)
             pl.when(jnp.logical_not(jnp.logical_or(near_left, run_left)))(send_sum_left)
+            pass_left = remote(cross_left_s, left_s.at[0], 9, to_other, 1)
+            pass_right = remote(cross_right_s, right_s.at[0], 10, to_other, 0)
+            started += [(relay_left, pass_left), (relay_right, pass_right)]
+
+            def pass_on(cross, onward):
+                cross.wait_recv()
+                onward.start()
+
+            pl.when(relay_left)(lambda: pass_on(cross_rightward, pass_left))
+            pl.when(relay_right)(lambda: pass_on(cross_leftward, pass_right))
             pl.when(cross_left)(rightward.wait_recv)
             pl.when(cross_right)(leftward.wait_recv)
+            for a in (0, 1, 4, 5):
+                node[a] = own(a, step)
             inner.wait_recv()
-            pl.when(cross_left)(cross_rightward.wait_recv)
-            pl.when(cross_right)(cross_leftward.wait_recv)
+            pl.when(jnp.logical_and(cross_left, phase == 1))(cross_rightward.wait_recv)
+            pl.when(jnp.logical_and(cross_right, phase == 1))(cross_leftward.wait_recv)
             sum_left.wait_recv()
             sum_right.wait_recv()
         else:
             pl.when(has_left)(rightward.wait_recv)
             pl.when(has_right)(leftward.wait_recv)
+            for a in (0, 1, 4, 5):
+                node[a] = own(a, step)
         node_vel = []
         for a in range(6):
-            full = [settled(a, c, mine, left_s.at[step], right_s.at[step], has_left, has_right) for c in range(4)]
-            v = velocity(full[0], full[1:])
+            mass, v = node[a]
             if step == 0:
                 other = [settled(a, c, other_s, cross_left_s, cross_right_s, cross_left, cross_right) for c in range(4)]
                 other_vel = velocity(other[0], other[1:])
                 coef = left_s[0, 0, 4] if a == 0 else right_s[0, 1, 4] if a == 5 else drag_ref[a - 1]
                 slip = [other_vel[e] - v[e] for e in range(3)]
                 rate = coef * jnp.sqrt(slip[0] * slip[0] + slip[1] * slip[1] + slip[2] * slip[2] + 0.25)
-                gain = rate / (1.0 + rate) * (other[0] / (full[0] + other[0] + 0.25))
+                gain = rate / (1.0 + rate) * (other[0] / (mass + other[0] + 0.25))
                 v = [v[e] + gain * slip[e] for e in range(3)]
             if a == 0:
                 v = [jnp.where(has_left, value, 0.0) for value in v]
@@ -492,7 +526,7 @@
             pltpu.VMEM((64, 128), F32),
             pltpu.VMEM((4, 8, 128), F32),
             pltpu.VMEM((NROW, 64, 128), F32),
-            pltpu.VMEM((2, 64, 128), jnp.int32),
+            pltpu.VMEM((2, 256, 128), F32),
             pltpu.VMEM((5, 136, 128), F32),
             pltpu.VMEM((5, 136, 128), F32),
             pltpu.VMEM((8, 256, 128), F32),
@@ -500,11 +534,11 @@
             pltpu.VMEM((4, 4, 8, 128), F32),
             pltpu.VMEM((2, 2, 5, 8, 128), F32),
             pltpu.VMEM((2, 2, 5, 8, 128), F32),
-            pltpu.VMEM((2, 4, 8, 128), F32),
-            pltpu.VMEM((2, 4, 8, 128), F32),
+            pltpu.VMEM((2, 5, 8, 128), F32),
+            pltpu.VMEM((2, 5, 8, 128), F32),
             pltpu.VMEM((6, 4, 8, 128), F32),
             pltpu.SemaphoreType.DMA((7,)),
-            pltpu.SemaphoreType.DMA((9,)),
+            pltpu.SemaphoreType.DMA((11,)),
             pltpu.SemaphoreType.DMA((9,)),
         ],
         compiler_params=pltpu.CompilerParams(

time: 24.4 us -> 23.4 us (0.959)
  Pallas kernels: 23.7 us -> 22.7 us
    pallas_call x1, Pallas kernels: 22.1 us -> 21.1 us  [local(): pl.pallas_call(nodes_kernel, out_shape=[jax.ShapeDtypeStruct(shape, kind)...]
where the time goes in v3:
time: 23.4 us; the launch traced here: 23.3 us
  Pallas kernels  22.7 us (97%)
  between operations  0.64 us (3%)
    pallas_call x1, Pallas kernels, local(): pl.pallas_call(nodes_kernel, out_shape=[jax.ShapeDtypeStruct(shape, kind)...  21.1 us
    pallas_call x1, Pallas kernels, local(): pl.pallas_call(particles_kernel, out_shape=[jax.ShapeDtypeStruct((3, 64,...  1.53 us

profile of v3, /device:TPU:24, one launch (start us, length us, event | category | flops | bytes accessed | tf_op | source)
XLA Modules:
  0.0 23.3 jit_solution(11642141412987839168)
XLA Ops:
  0.6 21.1 %shard_map.94 = (s32[64,128]{1,0:T(8,128)S(1)}, f32[64,128]{1,0:T(8,128)S(1)}, f32[3,64,128]{2,1,0:T(8,128)S(1)}, f32[3,64,128]{2,1,0:T(8,128)S(1)}, f32[64,128]...) custom-call(s32[64,128]{1,0:T(8,128)} %bitcast.10, ...), custom_call_target="tpu_custom_call" | custom-call | tf_op jit(solution)/shard_map/pallas_call | solution.py:516
  21.8 1.5 %shard_map.95 = (f32[3,64,128]{2,1,0:T(8,128)}, f32[3,64,128]{2,1,0:T(8,128)}, f32[64,128]{1,0:T(8,128)}) custom-call(s32[64,128]{1,0:T(8,128)S(1)} %get-tuple-element.16.cell_ref, f32[64,128]{1,0:T(8,128)S(1)} %get-tuple-element.17.live_s, f32[3,64,128]{2,1,0:T(8,128)S(1)} %get-tuple-element.18.frac_mid, f32[3,64,128]{2,1,0:T(8,128)S(1)} %get-tuple-element.19.vel_mid, ...), custom_call_target="tpu_custom_call" | custom-call | tf_op jit(solution)/shard_map/pallas_call | solution.py:548

commit v4 on v3

--- a/solution.py
+++ b/solution.py
@@ -10,6 +10,7 @@
 DT = 0.05
 MESH = pl.DeviceIdType.MESH
 RUN = 32
+ROW = 8
 
 FX, MASS, QX, QY, QZ, S2 = 0, 6, 7, 8, 9, 10
 NROW = 11
@@ -43,7 +44,7 @@
     frac_out, vel_out, stress_out = out
     sub8 = lax.broadcasted_iota(jnp.int32, (8, 128), 0)
 
-    def body(i, carry):
+    def body(i):
         for par in range(2):
             bz = 2 * i + par
             window = []
@@ -69,11 +70,8 @@
                 for c in range(3):
                     red_s[2 * c + by, at, :] = fz * u[c]
                 red_s[6 + by, at, :] = fz * u[3] + fzt * u[2]
-        return carry
-
-    lax.fori_loop(0, 16, body, 0, unroll=16)
-
-    for j in range(8):
+
+    def finish(j):
         here, cx, cy, cz, by, pos_x, pos_y = coords(cell_ref, frac, j)
         sums = []
         for c in range(4):
@@ -88,6 +86,12 @@
             f = frac[e, here, :]
             frac_out[e, here, :] = jnp.where(live, f + DT * sums[e], f)
             vel_out[e, here, :] = jnp.where(live, sums[e], vel[e, here, :])
+
+    for chunk in range(4):
+        for i in range(4 * chunk, 4 * chunk + 4):
+            body(i)
+        finish(chunk)
+        finish(chunk + 4)
 
 
 def nodes_kernel(
@@ -129,6 +133,7 @@
     load_sem,
     send_sem,
     recv_sem,
+    open_sem,
 ):
     n_space = lax.axis_size("space")
     me = lax.axis_index("space")
@@ -151,17 +156,37 @@
     relay_right = jnp.logical_and(cross_right, phase == 0)
     direct_left = jnp.logical_and(has_left, jnp.logical_not(jnp.logical_and(run_left, phase == 1)))
     direct_right = jnp.logical_and(has_right, jnp.logical_not(jnp.logical_and(run_right, phase == 1)))
+    row_left = jnp.logical_and(lax.rem(me, ROW) == 0, jnp.logical_not(run_left))
+    row_right = jnp.logical_and(lax.rem(me, ROW) == ROW - 1, jnp.logical_not(run_right))
+    raw_out_left = jnp.logical_or(run_left, jnp.logical_and(row_left, phase == 1))
+    raw_out_right = jnp.logical_or(run_right, jnp.logical_and(row_right, phase == 1))
+    out_left = jnp.logical_and(has_left, raw_out_left)
+    out_right = jnp.logical_and(has_right, raw_out_right)
+    in_left = jnp.logical_or(cross_left, jnp.logical_and(row_left, phase == 0))
+    in_right = jnp.logical_or(cross_right, jnp.logical_and(row_right, phase == 0))
     barrier = pltpu.get_barrier_semaphore()
 
-    def greet(target):
-        pl.semaphore_signal(barrier, inc=1, device_id=target, device_id_type=MESH)
-
-    greet(to_other)
+    def greet(target, sem=barrier):
+        pl.semaphore_signal(sem, inc=1, device_id=target, device_id_type=MESH)
+
+    def greet_across():
+        greet(to_other)
+        pl.when(in_left)(lambda: greet(to_cross_left))
+        pl.when(in_right)(lambda: greet(to_cross_right))
+
+    def answer_across():
+        greet(to_other, open_sem)
+        pl.when(cross_left)(lambda: greet(to_cross_left, open_sem))
+        pl.when(cross_right)(lambda: greet(to_cross_right, open_sem))
+
+    def count(*flags):
+        return sum(flag.astype(jnp.int32) for flag in flags)
+
     pl.when(direct_left)(lambda: greet(to_left))
     pl.when(direct_right)(lambda: greet(to_right))
-    pl.when(cross_left)(lambda: greet(to_cross_left))
-    pl.when(cross_right)(lambda: greet(to_cross_right))
-    greeted = 1 + sum(flag.astype(jnp.int32) for flag in (direct_left, direct_right, cross_left, cross_right))
+    pl.when(phase == 0)(greet_across)
+    greeted = count(direct_left, direct_right) + phase * (1 + count(out_left, out_right))
+    answered = 1 + count(cross_left, cross_right)
 
     loads = [
         pltpu.make_async_copy(src, dst, load_sem.at[k])
@@ -209,8 +234,8 @@
     slots = lax.broadcasted_iota(jnp.int32, (64, 128), 1).astype(F32)
     live_s[...] = jnp.where(slots < counts, 1.0, 0.0)
 
-    def prepare(frac, vel, stress):
-        for j in range(8):
+    def prepare(chunk, frac, vel, stress):
+        for j in (chunk, chunk + 4):
             here, cx, cy, cz, by, pos_x, pos_y = coords(cell_ref, frac, j)
             wx = factors(frac[0, here, :])
             wy = factors(frac[1, here, :])
@@ -248,8 +273,8 @@
             rows_s[QY, here, :] = m * vel[1, here, :] - s2 * pos_y
             rows_s[QZ, here, :] = m * vel[2, here, :] - s2 * (frac[2, here, :] - 0.5)
 
-    def deposit(step):
-        def body(i, carry):
+    def deposit(step, state):
+        def body(i):
             for par in range(2):
                 bz = 2 * i + par
                 plane = []
@@ -293,9 +318,11 @@
                         even_s[c, pl.ds(pl.multiple_of(8 * i, 8), 8), :] = out[8 * c : 8 * c + 8]
                     else:
                         odd_s[c, pl.ds(pl.multiple_of(8 * i + 8, 8), 8), :] = out[8 * c : 8 * c + 8]
-            return carry
-
-        lax.fori_loop(0, 16, body, 0, unroll=16)
+
+        for chunk in range(4):
+            prepare(chunk, *state)
+            for i in range(4 * chunk, 4 * chunk + 4):
+                body(i)
         fields = []
         row7 = (lax.broadcasted_iota(jnp.int32, (128, 128), 0) & 7) == 7
         row0 = (lax.broadcasted_iota(jnp.int32, (128, 128), 0) & 7) == 0
@@ -349,8 +376,7 @@
 
     for step in range(2):
         state = (frac_in, vel_in, stress_in) if step == 0 else (frac_mid, vel_mid, stress_mid)
-        prepare(*state)
-        deposit(step)
+        deposit(step, state)
         mine = grid_s.at[step]
         width = 5 if step == 0 else 4
         leftward = remote(mine.at[0:2, 0:width], right_s.at[step, :, 0:width], 2 * step, to_left)
@@ -363,9 +389,10 @@
             mine[0, 4] = zero8
             mine[5, 4] = zero8
             pl.semaphore_wait(barrier, greeted)
+            pl.when(phase == 1)(answer_across)
         if step == 0:
             inner = remote(mine.at[2:4, 0:4], other_s.at[2:4], 4, to_other)
-            inner.start()
+            pl.when(phase == 1)(inner.start)
         pl.when(go_left)(leftward.start)
         pl.when(go_right)(rightward.start)
         node = {a: own(a, step) for a in (2, 3)}
@@ -377,13 +404,19 @@
             sum_left = remote(edge_s.at[0:2], other_s.at[0:2], 7, to_other)
             sum_right = remote(edge_s.at[2:4], other_s.at[4:6], 8, to_other)
 
+            def begin_across():
+                pl.semaphore_wait(open_sem, answered)
+                inner.start()
+
+            pl.when(phase == 0)(begin_across)
+
             def send_raw(flag, run, cross, raw):
                 pl.when(flag)(cross.start)
                 pl.when(run)(raw.start)
 
-            send_raw(cross_left, run_left, cross_leftward, raw_left)
-            send_raw(cross_right, run_right, cross_rightward, raw_right)
-            started += [(cross_left, cross_leftward), (cross_right, cross_rightward)]
+            send_raw(out_left, raw_out_left, cross_leftward, raw_left)
+            send_raw(out_right, raw_out_right, cross_rightward, raw_right)
+            started += [(out_left, cross_leftward), (out_right, cross_rightward)]
             started += [(None, inner), (None, sum_left), (None, sum_right)]
 
             def send_sum_left():
@@ -402,8 +435,8 @@
 
             near_left = lax.rem(me, 2) == 1
             pl.when(near_left)(send_sum_left)
-            pl.when(jnp.logical_not(run_right))(send_sum_right)
-            pl.when(jnp.logical_not(jnp.logical_or(near_left, run_left)))(send_sum_left)
+            pl.when(jnp.logical_not(raw_out_right))(send_sum_right)
+            pl.when(jnp.logical_not(jnp.logical_or(near_left, raw_out_left)))(send_sum_left)
             pass_left = remote(cross_left_s, left_s.at[0], 9, to_other, 1)
             pass_right = remote(cross_right_s, right_s.at[0], 10, to_other, 0)
             started += [(relay_left, pass_left), (relay_right, pass_right)]
@@ -414,13 +447,13 @@
 
             pl.when(relay_left)(lambda: pass_on(cross_rightward, pass_left))
             pl.when(relay_right)(lambda: pass_on(cross_leftward, pass_right))
-            pl.when(cross_left)(rightward.wait_recv)
-            pl.when(cross_right)(leftward.wait_recv)
+            pl.when(out_left)(rightward.wait_recv)
+            pl.when(out_right)(leftward.wait_recv)
             for a in (0, 1, 4, 5):
                 node[a] = own(a, step)
             inner.wait_recv()
-            pl.when(jnp.logical_and(cross_left, phase == 1))(cross_rightward.wait_recv)
-            pl.when(jnp.logical_and(cross_right, phase == 1))(cross_leftward.wait_recv)
+            pl.when(jnp.logical_and(in_left, jnp.logical_not(relay_left)))(cross_rightward.wait_recv)
+            pl.when(jnp.logical_and(in_right, jnp.logical_not(relay_right)))(cross_leftward.wait_recv)
             sum_left.wait_recv()
             sum_right.wait_recv()
         else:
@@ -432,7 +465,7 @@
         for a in range(6):
             mass, v = node[a]
             if step == 0:
-                other = [settled(a, c, other_s, cross_left_s, cross_right_s, cross_left, cross_right) for c in range(4)]
+                other = [settled(a, c, other_s, cross_left_s, cross_right_s, in_left, in_right) for c in range(4)]
                 other_vel = velocity(other[0], other[1:])
                 coef = left_s[0, 0, 4] if a == 0 else right_s[0, 1, 4] if a == 5 else drag_ref[a - 1]
                 slip = [other_vel[e] - v[e] for e in range(3)]
@@ -540,6 +573,7 @@
             pltpu.SemaphoreType.DMA((7,)),
             pltpu.SemaphoreType.DMA((11,)),
             pltpu.SemaphoreType.DMA((9,)),
+            pltpu.SemaphoreType.REGULAR,
         ],
         compiler_params=pltpu.CompilerParams(
             collective_id=0, has_side_effects=True, vmem_limit_bytes=24 * 1024 * 1024

time: 23.4 us -> 23.3 us (level)
  the two profiles are of different devices: /device:TPU:24 before, /device:TPU:239 now
where the time goes in v4:
time: 23.3 us; the launch traced here: 23.1 us
  Pallas kernels  22.5 us (97%)
  between operations  0.64 us (3%)
    pallas_call x1, Pallas kernels, local(): pl.pallas_call(nodes_kernel, out_shape=[jax.ShapeDtypeStruct(shape, kind)...  21 us
    pallas_call x1, Pallas kernels, local(): pl.pallas_call(particles_kernel, out_shape=[jax.ShapeDtypeStruct((3, 64,...  1.53 us

profile of v4, /device:TPU:239, one launch (start us, length us, event | category | flops | bytes accessed | tf_op | source)
XLA Modules:
  0.0 23.1 jit_solution(8835402798917876464)
XLA Ops:
  0.6 21.0 %shard_map.94 = (s32[64,128]{1,0:T(8,128)S(1)}, f32[64,128]{1,0:T(8,128)S(1)}, f32[3,64,128]{2,1,0:T(8,128)S(1)}, f32[3,64,128]{2,1,0:T(8,128)S(1)}, f32[64,128]...) custom-call(s32[64,128]{1,0:T(8,128)} %bitcast.10, ...), custom_call_target="tpu_custom_call" | custom-call | tf_op jit(solution)/shard_map/pallas_call | solution.py:549
  21.6 1.5 %shard_map.95 = (f32[3,64,128]{2,1,0:T(8,128)}, f32[3,64,128]{2,1,0:T(8,128)}, f32[64,128]{1,0:T(8,128)}) custom-call(s32[64,128]{1,0:T(8,128)S(1)} %get-tuple-element.16.cell_ref, f32[64,128]{1,0:T(8,128)S(1)} %get-tuple-element.17.live_s, f32[3,64,128]{2,1,0:T(8,128)S(1)} %get-tuple-element.18.frac_mid, f32[3,64,128]{2,1,0:T(8,128)S(1)} %get-tuple-element.19.vel_mid, ...), custom_call_target="tpu_custom_call" | custom-call | tf_op jit(solution)/shard_map/pallas_call | solution.py:582

commit v5 on v4

--- a/solution.py
+++ b/solution.py
@@ -179,6 +179,10 @@
         pl.when(cross_left)(lambda: greet(to_cross_left, open_sem))
         pl.when(cross_right)(lambda: greet(to_cross_right, open_sem))
 
+    def enter():
+        pl.semaphore_wait(barrier, greeted)
+        answer_across()
+
     def count(*flags):
         return sum(flag.astype(jnp.int32) for flag in flags)
 
@@ -320,6 +324,8 @@
                         odd_s[c, pl.ds(pl.multiple_of(8 * i + 8, 8), 8), :] = out[8 * c : 8 * c + 8]
 
         for chunk in range(4):
+            if step == 0 and chunk == 2:
+                pl.when(phase == 1)(enter)
             prepare(chunk, *state)
             for i in range(4 * chunk, 4 * chunk + 4):
                 body(i)
@@ -388,8 +394,7 @@
                 mine[a, 4] = drag_ref[a - 1]
             mine[0, 4] = zero8
             mine[5, 4] = zero8
-            pl.semaphore_wait(barrier, greeted)
-            pl.when(phase == 1)(answer_across)
+            pl.when(phase == 0)(lambda: pl.semaphore_wait(barrier, greeted))
         if step == 0:
             inner = remote(mine.at[2:4, 0:4], other_s.at[2:4], 4, to_other)
             pl.when(phase == 1)(inner.start)

time: 23.3 us -> 23.3 us (level)
  the two profiles are of different devices: /device:TPU:239 before, /device:TPU:231 now
where the time goes in v5:
time: 23.3 us; the launch traced here: 23.2 us
  Pallas kernels  22.5 us (97%)
  between operations  0.64 us (3%)
    pallas_call x1, Pallas kernels, local(): pl.pallas_call(nodes_kernel, out_shape=[jax.ShapeDtypeStruct(shape, kind)...  21 us
    pallas_call x1, Pallas kernels, local(): pl.pallas_call(particles_kernel, out_shape=[jax.ShapeDtypeStruct((3, 64,...  1.53 us

profile of v5, /device:TPU:231, one launch (start us, length us, event | category | flops | bytes accessed | tf_op | source)
XLA Modules:
  0.0 23.2 jit_solution(10602839679815529722)
XLA Ops:
  0.6 21.0 %shard_map.94 = (s32[64,128]{1,0:T(8,128)S(1)}, f32[64,128]{1,0:T(8,128)S(1)}, f32[3,64,128]{2,1,0:T(8,128)S(1)}, f32[3,64,128]{2,1,0:T(8,128)S(1)}, f32[64,128]...) custom-call(s32[64,128]{1,0:T(8,128)} %bitcast.10, ...), custom_call_target="tpu_custom_call" | custom-call | tf_op jit(solution)/shard_map/pallas_call | solution.py:554
  21.6 1.5 %shard_map.95 = (f32[3,64,128]{2,1,0:T(8,128)}, f32[3,64,128]{2,1,0:T(8,128)}, f32[64,128]{1,0:T(8,128)}) custom-call(s32[64,128]{1,0:T(8,128)S(1)} %get-tuple-element.16.cell_ref, f32[64,128]{1,0:T(8,128)S(1)} %get-tuple-element.17.live_s, f32[3,64,128]{2,1,0:T(8,128)S(1)} %get-tuple-element.18.frac_mid, f32[3,64,128]{2,1,0:T(8,128)S(1)} %get-tuple-element.19.vel_mid, ...), custom_call_target="tpu_custom_call" | custom-call | tf_op jit(solution)/shard_map/pallas_call | solution.py:587

commit v6 on v3

--- a/solution.py
+++ b/solution.py
@@ -43,7 +43,7 @@
     frac_out, vel_out, stress_out = out
     sub8 = lax.broadcasted_iota(jnp.int32, (8, 128), 0)
 
-    def body(i, carry):
+    def body(i):
         for par in range(2):
             bz = 2 * i + par
             window = []
@@ -69,11 +69,8 @@
                 for c in range(3):
                     red_s[2 * c + by, at, :] = fz * u[c]
                 red_s[6 + by, at, :] = fz * u[3] + fzt * u[2]
-        return carry
-
-    lax.fori_loop(0, 16, body, 0, unroll=16)
-
-    for j in range(8):
+
+    def finish(j):
         here, cx, cy, cz, by, pos_x, pos_y = coords(cell_ref, frac, j)
         sums = []
         for c in range(4):
@@ -88,6 +85,12 @@
             f = frac[e, here, :]
             frac_out[e, here, :] = jnp.where(live, f + DT * sums[e], f)
             vel_out[e, here, :] = jnp.where(live, sums[e], vel[e, here, :])
+
+    for chunk in range(4):
+        for i in range(4 * chunk, 4 * chunk + 4):
+            body(i)
+        finish(chunk)
+        finish(chunk + 4)
 
 
 def nodes_kernel(
@@ -209,8 +212,8 @@
     slots = lax.broadcasted_iota(jnp.int32, (64, 128), 1).astype(F32)
     live_s[...] = jnp.where(slots < counts, 1.0, 0.0)
 
-    def prepare(frac, vel, stress):
-        for j in range(8):
+    def prepare(chunk, frac, vel, stress):
+        for j in (chunk, chunk + 4):
             here, cx, cy, cz, by, pos_x, pos_y = coords(cell_ref, frac, j)
             wx = factors(frac[0, here, :])
             wy = factors(frac[1, here, :])
@@ -248,8 +251,8 @@
             rows_s[QY, here, :] = m * vel[1, here, :] - s2 * pos_y
             rows_s[QZ, here, :] = m * vel[2, here, :] - s2 * (frac[2, here, :] - 0.5)
 
-    def deposit(step):
-        def body(i, carry):
+    def deposit(step, state):
+        def body(i):
             for par in range(2):
                 bz = 2 * i + par
                 plane = []
@@ -293,9 +296,11 @@
                         even_s[c, pl.ds(pl.multiple_of(8 * i, 8), 8), :] = out[8 * c : 8 * c + 8]
                     else:
                         odd_s[c, pl.ds(pl.multiple_of(8 * i + 8, 8), 8), :] = out[8 * c : 8 * c + 8]
-            return carry
-
-        lax.fori_loop(0, 16, body, 0, unroll=16)
+
+        for chunk in range(4):
+            prepare(chunk, *state)
+            for i in range(4 * chunk, 4 * chunk + 4):
+                body(i)
         fields = []
         row7 = (lax.broadcasted_iota(jnp.int32, (128, 128), 0) & 7) == 7
         row0 = (lax.broadcasted_iota(jnp.int32, (128, 128), 0) & 7) == 0
@@ -349,8 +354,7 @@
 
     for step in range(2):
         state = (frac_in, vel_in, stress_in) if step == 0 else (frac_mid, vel_mid, stress_mid)
-        prepare(*state)
-        deposit(step)
+        deposit(step, state)
         mine = grid_s.at[step]
         width = 5 if step == 0 else 4
         leftward = remote(mine.at[0:2, 0:width], right_s.at[step, :, 0:width], 2 * step, to_left)

time: 23.4 us -> 23.4 us (level)
  no operation moved by 1% of the time
where the time goes in v6:
time: 23.4 us; the launch traced here: 23.3 us
  Pallas kernels  22.7 us (97%)
  between operations  0.64 us (3%)
    pallas_call x1, Pallas kernels, local(): pl.pallas_call(nodes_kernel, out_shape=[jax.ShapeDtypeStruct(shape, kind)...  21.1 us
    pallas_call x1, Pallas kernels, local(): pl.pallas_call(particles_kernel, out_shape=[jax.ShapeDtypeStruct((3, 64,...  1.53 us

profile of v6, /device:TPU:24, one launch (start us, length us, event | category | flops | bytes accessed | tf_op | source)
XLA Modules:
  0.0 23.3 jit_solution(11642141412987839168)
XLA Ops:
  0.6 21.1 %shard_map.94 = (s32[64,128]{1,0:T(8,128)S(1)}, f32[64,128]{1,0:T(8,128)S(1)}, f32[3,64,128]{2,1,0:T(8,128)S(1)}, f32[3,64,128]{2,1,0:T(8,128)S(1)}, f32[64,128]...) custom-call(s32[64,128]{1,0:T(8,128)} %bitcast.10, ...), custom_call_target="tpu_custom_call" | custom-call | tf_op jit(solution)/shard_map/pallas_call | solution.py:520
  21.8 1.5 %shard_map.95 = (f32[3,64,128]{2,1,0:T(8,128)}, f32[3,64,128]{2,1,0:T(8,128)}, f32[64,128]{1,0:T(8,128)}) custom-call(s32[64,128]{1,0:T(8,128)S(1)} %get-tuple-element.16.cell_ref, f32[64,128]{1,0:T(8,128)S(1)} %get-tuple-element.17.live_s, f32[3,64,128]{2,1,0:T(8,128)S(1)} %get-tuple-element.18.frac_mid, f32[3,64,128]{2,1,0:T(8,128)S(1)} %get-tuple-element.19.vel_mid, ...), custom_call_target="tpu_custom_call" | custom-call | tf_op jit(solution)/shard_map/pallas_call | solution.py:552
